TPU v7x, 128 devices: a whole 4x4x4 slice. The times are simulated.
128 devices in a mesh: dp: 4 (over x), frame: 4 (over z), expert: 8 (over y, core).
Axes of the slice: x: 4, y: 4, z: 4, core: 2. Of those that a mesh axis runs over, the one named last changes fastest.
Arguments:
- queries: bfloat16 [16384, 2048], P(('dp', 'frame'), 'expert'), parts along dimension 0, may hold values from -8 to 8
- keys: bfloat16 [16384, 2048], P(('dp', 'frame'), 'expert'), parts along dimension 0, may hold values from -8 to 8
- values: bfloat16 [16384, 2048], P(('dp', 'frame'), 'expert'), parts along dimension 0, may hold values from -6 to 6
- hidden_state: bfloat16 [16384, 4096], P(('dp', 'frame', 'expert')), parts along dimension 0, may hold values from -60 to 60
- out_grad: bfloat16 [16384, 4096], P(('dp', 'frame', 'expert')), parts along dimension 0, may hold values from -6 to 6
- stored_pre: bfloat16 [16384, 2, 2, 2048], P(('dp', 'frame', 'expert')), parts along dimension 0, may hold values from -6 to 6
- expert_ids: int32 [16384, 2], P(('dp', 'frame', 'expert')), parts along dimension 0, may hold values from 0 to 7, as said below
- gate_weights: float32 [16384, 2], P(('dp', 'frame', 'expert')), parts along dimension 0, may hold values from 0.25 to 1
- w_gate: bfloat16 [8, 4096, 2048], P('expert', None, 'frame'), may hold values from -0.09375 to 0.09375
- w_up: bfloat16 [8, 4096, 2048], P('expert', None, 'frame'), may hold values from -0.09375 to 0.09375
- w_down: bfloat16 [8, 2048, 4096], P('expert', 'frame'), may hold values from -0.125 to 0.125
Outputs:
- residual_grad: bfloat16 [16384, 4096], P(('dp', 'frame', 'expert')), parts along dimension 0
- query_grad: bfloat16 [16384, 2048], P(('dp', 'frame'), 'expert'), parts along dimension 0
- key_grad: bfloat16 [16384, 2048], P(('dp', 'frame'), 'expert'), parts along dimension 0
- value_grad: bfloat16 [16384, 2048], P(('dp', 'frame'), 'expert'), parts along dimension 0
There are 4 independent parts, one for each index of `dp`. A program takes and returns all parts, laid end to end along the dimension named above; an argument that names none is the same for every part. Nothing has to cross between parts.
Inputs may be any that keep to these rules, and one draw needn't show every extreme that they name: `expert_ids`: each token names 2 different experts. In the tokens of one device (aligned blocks of 128 rows) no expert is named more than 36 times; in each span one expert is named exactly 36 times in every block of that span.
All inputs are finite; a program needn't handle non-finite values.
Results may differ from a plain program's by a relative error of at most 0.015.
Values may be sent and summed in bfloat16 or wider, within the bound.
A program may use at most 192 MiB of HBM per device.

v0:
```python
import functools

import jax
import jax.numpy as jnp
from jax import lax
from jax.experimental import pallas as pl
from jax.experimental.pallas import tpu as pltpu
from jax.sharding import PartitionSpec as P

HD = 128
N_EXP = 8
N_FRAME = 4
MAIN = 16
BF = jnp.bfloat16
F32 = jnp.float32
MESH = pl.DeviceIdType.MESH
VMEM_LIMIT = 63 * 1024 * 1024


def dot_nn(a, b):
    return lax.dot_general(a, b, (((1,), (0,)), ((), ())), preferred_element_type=F32)


def dot_nt(a, b):
    return lax.dot_general(a, b, (((1,), (1,)), ((), ())), preferred_element_type=F32)


ZF = 2
RF = 1


def moe_kernel(
    meta_ref, og_ref, st_ref, hs_ref, wd_hbm, wg_hbm, wu_hbm, k_hbm, v_hbm,
    resid_ref, gout_ref, k_far, v_far,
    wd, wg, wu, rows, stored, hid, grads, ysend, yrecv, zrecv,
    half_in, full_in, dhalf_in, dfull_in, dense, amat, emat, atmat, etmat, raw, meta_in,
    w_sem, ys_sem, yr_sem, zs_sem, zr_sem, ag_s, ag_r, fw_s, fw_r, st_s, st_r,
    ha_s, ha_r, fu_s, fu_r, go_s, go_r, me_s, me_r, ra_s, ra_r, rf_s, rf_r,
    dh_s, dh_r, df_s, df_r, kv_s, kv_r,
):
    me = lax.axis_index("expert")
    fr = lax.axis_index("frame")
    left = lax.rem(fr + 3, 4)
    right = lax.rem(fr + 1, 4)
    opposite = lax.rem(fr + 2, 4)
    toks, width = og_ref.shape
    cw = width // 4
    ext = cw // 4
    ff = hid.shape[2]
    n_rows = rows.shape[2]
    half = n_rows // 2
    thalf = toks // 2
    n_blk = N_EXP * MAIN
    n_extra = 3 * ZF

    def chunk_at(c):
        return pl.ds(pl.multiple_of(c * cw, cw), cw)

    def to_frame(src, dst, ss, rs, dest):
        return pltpu.make_async_remote_copy(
            src_ref=src, dst_ref=dst, send_sem=ss, recv_sem=rs,
            device_id={"frame": dest}, device_id_type=MESH)

    def to_side(src, dst, ss, rs, side):
        return to_frame(src, dst, ss, rs, right if side == 0 else left)

    def to_expert(src, dst, ss, rs, dest):
        return pltpu.make_async_remote_copy(
            src_ref=src, dst_ref=dst, send_sem=ss, recv_sem=rs,
            device_id={"expert": dest}, device_id_type=MESH)

    barrier = pltpu.get_barrier_semaphore()
    for d in range(1, N_EXP):
        pl.semaphore_signal(barrier, inc=1, device_id={"expert": lax.rem(me + d, N_EXP)}, device_id_type=MESH)
    for dest in (left, right, opposite):
        pl.semaphore_signal(barrier, inc=1, device_id={"frame": dest}, device_id_type=MESH)

    w_copies = [pltpu.make_async_copy(wd_hbm.at[:, pl.ds(c * cw, cw)], wd.at[c], w_sem.at[c]) for c in range(4)]
    w_copies += [pltpu.make_async_copy(wg_hbm, wg, w_sem.at[4]), pltpu.make_async_copy(wu_hbm, wu, w_sem.at[5])]
    for copy in w_copies:
        copy.start()

    def raw_copy(c, side):
        return to_side(og_ref.at[:, chunk_at(c)], raw.at[side, c], ra_s.at[c, side], ra_r.at[c, side], side)

    def raw_pass(c, side):
        part = pl.ds(side * thalf, thalf)
        return to_side(raw.at[side, c, part], raw.at[2, c, part], rf_s.at[c, side], rf_r.at[c, side], side)

    meta_copies = [
        to_frame(meta_ref, meta_in.at[0], me_s.at[0], me_r.at[0], right),
        to_frame(meta_ref, meta_in.at[1], me_s.at[1], me_r.at[1], left),
        to_frame(meta_ref, meta_in.at[2], me_s.at[2], me_r.at[2], opposite),
    ]
    pl.semaphore_wait(barrier, N_EXP + 2)
    for copy in meta_copies:
        copy.start()
    for c in range(ZF):
        for side in range(2):
            raw_copy(c, side).start()

    earlier_mask = (
        lax.broadcasted_iota(jnp.int32, (toks, toks), 0) < lax.broadcasted_iota(jnp.int32, (toks, toks), 1)
    ).astype(F32).astype(BF)
    expert_iota = lax.broadcasted_iota(jnp.int32, (N_EXP, toks), 0)
    main_iota = lax.broadcasted_iota(jnp.int32, (2 * n_blk, toks), 0)
    ext_iota = lax.broadcasted_iota(jnp.int32, (n_blk, toks), 0)

    def routing(b, meta):
        base = jnp.zeros((N_EXP, 1), F32)
        main_sum = jnp.zeros(main_iota.shape, F32)
        ext_sum = [jnp.zeros(ext_iota.shape, F32) for _ in range(4)]
        for k in range(2):
            rel = (meta[k:k + 1, :].astype(jnp.int32) - me + N_EXP) & (N_EXP - 1)
            hit = (expert_iota == rel).astype(F32)
            earlier = dot_nn(hit.astype(BF), earlier_mask) + base
            slot = jnp.sum(hit * earlier, axis=0, keepdims=True).astype(jnp.int32)
            base = base + jnp.sum(hit, axis=1, keepdims=True)
            main_at = jnp.where(slot < 32, (slot >> 4) * n_blk + rel * MAIN + (slot & 15), -1)
            ext_at = jnp.where(slot < 32, -1000, rel * MAIN + slot - 32)
            main_k = (main_iota == main_at).astype(F32)
            amat[:, pl.ds(k * toks, toks)] = main_k.astype(BF)
            main_sum = main_sum + main_k
            for j in range(4):
                ext_k = (ext_iota == ext_at + 4 * j).astype(F32)
                emat[j, :, pl.ds(k * toks, toks)] = ext_k.astype(BF)
                ext_sum[j] = ext_sum[j] + ext_k
        atmat[b] = main_sum.T.astype(BF)
        for j in range(4):
            etmat[b, j] = ext_sum[j].T.astype(BF)
        return meta.T

    def pack_pairs(slot, at, pairs):
        main = dot_nn(amat[...], pairs).astype(BF)
        extra = dot_nn(emat[0], pairs[:, :ext])
        for j in range(1, 4):
            extra = extra + dot_nn(emat[j], pairs[:, j * ext:(j + 1) * ext])
        extra = extra.astype(BF)
        for lo, w, part in ((0, cw, main[:n_blk]), (cw, cw, main[n_blk:]), (2 * cw, ext, extra)):
            ysend[slot, :, pl.ds(lo, w)] = part
            yrecv[at, pl.ds(0, MAIN), pl.ds(lo, w)] = part[:MAIN]

    def pack_tokens(slot, at, x, weights):
        x = x.astype(F32)
        pack_pairs(slot, at, jnp.concatenate(
            [(weights[:, 2:3] * x).astype(BF), (weights[:, 3:4] * x).astype(BF)], axis=0))

    def y_copy(slot, at, d):
        return to_expert(
            ysend.at[slot, pl.ds(MAIN * d, MAIN)], yrecv.at[at, pl.ds(MAIN * d, MAIN)],
            ys_sem.at[at, d], yr_sem.at[at, d], lax.rem(me + d, N_EXP))

    def y_start(slot, at):
        for d in range(1, N_EXP):
            y_copy(slot, at, d).start()

    def y_sent(slot, at):
        for d in range(1, N_EXP):
            y_copy(slot, at, d).wait_send()

    own_weights = routing(0, meta_ref[...])

    def build_rows(c, carry):
        pack_tokens(c, c, og_ref[:, chunk_at(c)], own_weights)
        y_start(c, c)
        return carry

    def build_stored(c, carry):
        f = lax.rem(fr + c, 4)
        parts = []
        for k in range(2):
            parts.append(jnp.concatenate(
                [st_ref[:, pl.ds(pl.multiple_of((k * 2 + kind) * 4 * ff + f * ff, ff), ff)] for kind in range(2)], axis=1))
        pack_pairs(4 + c, 4 + c, jnp.concatenate(parts, axis=0))
        y_start(4 + c, 4 + c)
        return carry

    lax.fori_loop(ZF, 4, build_rows, 0)
    lax.fori_loop(0, 4, build_stored, 0)
    lax.fori_loop(0, ZF, build_rows, 0)

    sel_r = lax.broadcasted_iota(jnp.int32, (4 * N_EXP, n_blk), 0)
    sel_c = lax.broadcasted_iota(jnp.int32, (4 * N_EXP, n_blk), 1)
    selt_r = lax.broadcasted_iota(jnp.int32, (n_blk, 4 * N_EXP), 1)
    selt_c = lax.broadcasted_iota(jnp.int32, (n_blk, 4 * N_EXP), 0)

    def unpack(slot, at, dst):
        for d in range(1, N_EXP):
            y_copy(slot, at, d).wait_recv()
        dst[pl.ds(0, n_blk), :] = yrecv[at, :, pl.ds(0, cw)]
        dst[pl.ds(n_blk, n_blk), :] = yrecv[at, :, pl.ds(cw, cw)]
        extra = yrecv[at, :, pl.ds(2 * cw, ext)]
        for j in range(4):
            sel = (sel_c == (sel_r >> 2) * MAIN + 4 * j + (sel_r & 3)).astype(F32).astype(BF)
            dst[pl.ds(2 * n_blk, 4 * N_EXP), pl.ds(j * ext, ext)] = dot_nn(sel, extra).astype(BF)

    def ag_copy(c, side):
        return to_side(rows.at[0, c], rows.at[1 + side, c], ag_s.at[c, side], ag_r.at[c, side], side)

    def fw_copy(c, side):
        part = pl.ds(side * half, half)
        return to_side(rows.at[1 + side, c, part], rows.at[3, c, part], fw_s.at[c, side], fw_r.at[c, side], side)

    def add_hidden(b, c):
        hid[b] += dot_nt(rows[b, c], wd[c])

    for c in range(ZF):
        for side in range(2):
            raw_copy(c, side).wait_recv()
            raw_pass(c, side).start()

    def own_rows(c, carry):
        unpack(c, c, rows.at[0, c])
        ag_copy(c, 0).start()
        ag_copy(c, 1).start()
        return carry

    lax.fori_loop(ZF, 4, own_rows, 0)

    for copy in meta_copies:
        copy.wait_recv()
    for b in range(1, 4):
        weights = routing(b, meta_in[b - 1])
        for c in range(ZF):
            i = (b - 1) * ZF + c
            if b == 3:
                for side in range(2):
                    raw_pass(c, side).wait_recv()
            y_sent(i, i)
            pack_tokens(i, 8 + i, raw[b - 1, c], weights)
            y_start(i, 8 + i)

    hid[...] = jnp.zeros_like(hid)
    for copy in w_copies[:4]:
        copy.wait()

    def next_rows(c, carry):
        for side in range(2):
            ag_copy(c, side).wait_recv()
            fw_copy(c, side).start()
        add_hidden(0, c)
        add_hidden(1, c)
        add_hidden(2, c)
        return carry

    lax.fori_loop(ZF, 4, next_rows, 0)

    def own_stored(c, carry):
        unpack(4 + c, 4 + c, grads.at[c])
        return carry

    lax.fori_loop(0, 4, own_stored, 0)
    st_copies = [
        to_frame(grads.at[1], stored.at[0], st_s.at[0], st_r.at[0], right),
        to_frame(grads.at[3], stored.at[1], st_s.at[1], st_r.at[1], left),
        to_frame(grads.at[2], stored.at[2], st_s.at[2], st_r.at[2], opposite),
    ]
    for i in (2, 0, 1):
        st_copies[i].start()

    for c in range(ZF):
        unpack(c, c, rows.at[0, c])
        add_hidden(0, c)

    def far_rows(c, carry):
        for side in range(2):
            fw_copy(c, side).wait_recv()
        add_hidden(3, c)
        return carry

    lax.fori_loop(ZF, 4, far_rows, 0)

    for b in range(1, 4):
        for c in range(ZF):
            i = (b - 1) * ZF + c
            unpack(i, 8 + i, rows.at[b, c])
            add_hidden(b, c)

    def kv_near(i, side):
        src, dst = ((k_hbm, k_far), (v_hbm, v_far))[i]
        return to_side(src, dst.at[2 * side], kv_s.at[i, side], kv_r.at[i, side], side)

    def kv_pass(i):
        dst = (k_far, v_far)[i]
        return to_side(dst.at[2 * i], dst.at[1], kv_s.at[i, 2], kv_r.at[i, 2], i)

    @pl.when(fr <= 2)
    def _():
        kv_near(0, 0).start()

    @pl.when(fr == 0)
    def _():
        kv_near(0, 1).start()

    def hidden_to_grads(b, src):
        h = hid[b]
        g = src[:, pl.ds(0, ff)].astype(F32)
        u = src[:, pl.ds(ff, ff)].astype(F32)
        s = 1.0 / (1.0 + jnp.exp(-g))
        gate = (h * u * s * (1.0 + g * (1.0 - s))).astype(BF)
        up = (h * g * s).astype(BF)
        grads[b, :, pl.ds(0, ff)] = gate
        grads[b, :, pl.ds(ff, ff)] = up

    for i in (2, 0, 1):
        st_copies[i].wait()
    for b in (3, 2, 1, 0):
        hidden_to_grads(b, grads.at[0] if b == 0 else stored.at[b - 1])

    for copy in w_copies[4:]:
        copy.wait()

    def term(b, c):
        at = chunk_at(c)
        return dot_nt(grads[b, :, pl.ds(0, ff)], wg[at, :]) + dot_nt(grads[b, :, pl.ds(ff, ff)], wu[at, :])

    def ha_copy(c, side):
        return to_side(rows.at[3, c, pl.ds(side * half, half)], half_in.at[side, c - RF],
                       ha_s.at[c, side], ha_r.at[c, side], side)

    def fu_copy(c, side):
        return to_side(rows.at[2 - side, c], full_in.at[side, c - RF], fu_s.at[c, side], fu_r.at[c, side], side)

    def far_terms(c, carry):
        rows[3, c] = term(3, c).astype(BF)
        for side in range(2):
            ha_copy(c, side).start()
        return carry

    lax.fori_loop(RF, 4, far_terms, 0)

    def settle(i, carry):
        y_sent(lax.rem(i, 8), i)
        return carry

    lax.fori_loop(n_extra, 8 + n_extra, settle, 0)

    def z_copy(slot, d):
        return to_expert(
            ysend.at[slot, pl.ds(MAIN * d, MAIN)], zrecv.at[slot, pl.ds(MAIN * d, MAIN)],
            zs_sem.at[slot, d], zr_sem.at[slot, d], lax.rem(me + N_EXP - d, N_EXP))

    def send_back(slot, total):
        extra = jnp.zeros((n_blk, ext), F32)
        for j in range(4):
            sel = (selt_c == (selt_r >> 2) * MAIN + 4 * j + (selt_r & 3)).astype(F32).astype(BF)
            extra = extra + dot_nn(sel, total[2 * n_blk:, j * ext:(j + 1) * ext])
        extra = extra.astype(BF)
        for lo, w, part in ((0, cw, total[:n_blk]), (cw, cw, total[n_blk:2 * n_blk]), (2 * cw, ext, extra)):
            ysend[slot, :, pl.ds(lo, w)] = part
            zrecv[slot, pl.ds(0, MAIN), pl.ds(lo, w)] = part[:MAIN]
        for d in range(1, N_EXP):
            z_copy(slot, d).start()

    def tokens_of(slot, b):
        for d in range(1, N_EXP):
            z_copy(slot, d).wait_recv()
        got = dot_nn(atmat[b, :, pl.ds(0, n_blk)], zrecv[slot, :, pl.ds(0, cw)])
        got = got + dot_nn(atmat[b, :, pl.ds(n_blk, n_blk)], zrecv[slot, :, pl.ds(cw, cw)])
        extra = zrecv[slot, :, pl.ds(2 * cw, ext)]
        return got + jnp.concatenate([dot_nn(etmat[b, j], extra) for j in range(4)], axis=1)

    for c in range(RF):
        for b in (3, 2, 1, 0):
            send_back(4 + 4 * c + b, term(b, c).astype(BF))

    def near_terms(c, carry):
        for side in range(2):
            @pl.when(c >= ZF)
            def _():
                fw_copy(c, 1 - side).wait_send()
            part = term(2 - side, c)
            ha_copy(c, side).wait_recv()
            lo = side * half
            rows[2 - side, c, pl.ds(half - lo, half)] = part[half - lo:half - lo + half].astype(BF)
            rows[2 - side, c, pl.ds(lo, half)] = (
                part[lo:lo + half].astype(BF).astype(F32) + half_in[side, c - RF].astype(F32)).astype(BF)
            fu_copy(c, side).start()
        return carry

    lax.fori_loop(RF, 4, near_terms, 0)

    def put_moe(c, got):
        hid[c, pl.ds(0, toks), :] = got[:, :cw // 2]
        hid[c, pl.ds(toks, toks), :] = got[:, cw // 2:]

    def get_moe(c):
        return jnp.concatenate([hid[c, pl.ds(0, toks), :], hid[c, pl.ds(toks, toks), :]], axis=1)

    def dh_copy(c, side):
        part = pl.ds(side * thalf, thalf)
        return to_side(dense.at[c, 2, part], dhalf_in.at[side, c], dh_s.at[c, side], dh_r.at[c, side], side)

    def df_copy(c, side):
        return to_side(dense.at[c, 1 - side], dfull_in.at[side, c], df_s.at[c, side], df_r.at[c, side], side)

    for c in range(RF):
        dense[c, 2] = tokens_of(4 + 4 * c + 3, 3).astype(BF)
        for side in range(2):
            dh_copy(c, side).start()
        for side in range(2):
            b = 2 - side
            dense[c, b - 1] = tokens_of(4 + 4 * c + b, b).astype(BF)
        for side in range(2):
            b = 2 - side
            part = pl.ds(side * thalf, thalf)
            dh_copy(c, side).wait_recv()
            dense[c, b - 1, part] = (
                dense[c, b - 1, part].astype(F32) + dhalf_in[side, c].astype(F32)).astype(BF)
            df_copy(c, side).start()
        put_moe(c, tokens_of(4 + 4 * c, 0))

    @pl.when(fr >= 1)
    def _():
        kv_near(0, 0).wait_recv()

    @pl.when((fr == 1) | (fr == 2))
    def _():
        kv_pass(0).start()

    @pl.when(fr <= 2)
    def _():
        kv_near(1, 0).start()

    @pl.when(fr <= 1)
    def _():
        kv_near(1, 1).start()

    def own_terms(c, carry):
        part = term(0, c).astype(BF).astype(F32)
        for side in range(2):
            fu_copy(c, side).wait_recv()
        send_back(c, (part + full_in[0, c - RF].astype(F32) + full_in[1, c - RF].astype(F32)).astype(BF))
        return carry

    lax.fori_loop(RF, 4, own_terms, 0)

    @pl.when((fr == 3) | (fr == 0))
    def _():
        kv_near(1, 1).wait_recv()
        kv_pass(1).start()

    def square_sum(c, acc):
        x = hs_ref[:, chunk_at(c)].astype(F32)
        return acc + jnp.sum(x * x, axis=1, keepdims=True)

    inv = lax.rsqrt(lax.fori_loop(0, 4, square_sum, jnp.zeros((toks, 1), F32)) / width + 1e-6)

    def combine(c, acc):
        got = tokens_of(c, 0)
        put_moe(c, got)
        return acc + jnp.sum(got * hs_ref[:, chunk_at(c)].astype(F32), axis=1, keepdims=True)

    mean = lax.fori_loop(RF, 4, combine, jnp.zeros((toks, 1), F32))
    for c in range(RF):
        at = pl.ds(c * cw, cw)
        got = get_moe(c)
        for side in range(2):
            df_copy(c, side).wait_recv()
            got = got + dfull_in[side, c].astype(F32)
        put_moe(c, got)
        mean = mean + jnp.sum(got * hs_ref[:, at].astype(F32), axis=1, keepdims=True)
    mean = mean * inv / width

    def residual(c, carry):
        at = chunk_at(c)
        n = hs_ref[:, at].astype(F32) * inv
        resid_ref[:, at] = (og_ref[:, at].astype(F32) + inv * (get_moe(c) - n * mean)).astype(BF)
        return carry

    hw = gout_ref.shape[1]
    own_at = pl.ds(pl.multiple_of(me * toks, toks), toks)

    def go_copy(d):
        dest = lax.rem(me + d, N_EXP)
        return to_expert(
            resid_ref.at[:, pl.ds(pl.multiple_of(dest * hw, hw), hw)], gout_ref.at[own_at],
            go_s.at[d], go_r.at[d], dest)

    lax.fori_loop(0, 2, residual, 0)
    for d in range(1, N_EXP):
        go_copy(d).start()
    gout_ref[own_at, :] = resid_ref[:, pl.ds(pl.multiple_of(me * hw, hw), hw)]
    lax.fori_loop(2, 4, residual, 0)

    @pl.when(fr <= 2)
    def _():
        kv_near(0, 0).wait_send()
        kv_near(1, 0).wait_send()

    @pl.when(fr == 0)
    def _():
        kv_near(0, 1).wait_send()

    @pl.when(fr <= 1)
    def _():
        kv_near(1, 1).wait_send()

    @pl.when((fr == 1) | (fr == 2))
    def _():
        kv_pass(0).wait_send()

    @pl.when((fr == 3) | (fr == 0))
    def _():
        kv_pass(1).wait_send()

    @pl.when(fr >= 1)
    def _():
        kv_near(1, 0).wait_recv()

    @pl.when(fr == 3)
    def _():
        kv_near(0, 1).wait_recv()

    @pl.when(fr >= 2)
    def _():
        kv_pass(0).wait_recv()
        kv_pass(1).wait_recv()

    for copy in meta_copies:
        copy.wait_send()
    for c in range(ZF):
        for side in range(2):
            raw_copy(c, side).wait_send()
            raw_pass(c, side).wait_send()
    for c in range(RF):
        for side in range(2):
            dh_copy(c, side).wait_send()
            df_copy(c, side).wait_send()

    def drain(c, carry):
        for side in range(2):
            ag_copy(c, side).wait_send()
        return carry

    def drain_back(c, carry):
        for side in range(2):
            ha_copy(c, side).wait_send()
            fu_copy(c, side).wait_send()
        return carry

    def drain_z(slot, carry):
        for d in range(1, N_EXP):
            z_copy(slot, d).wait_send()
        return carry

    lax.fori_loop(ZF, 4, drain, 0)
    lax.fori_loop(RF, 4, drain_back, 0)
    lax.fori_loop(RF, 4 + 4 * RF, drain_z, 0)
    for c in range(ZF, RF):
        for side in range(2):
            fw_copy(c, side).wait_send()
    for d in range(1, N_EXP):
        go_copy(d).wait()


def moe_call(meta, out_grad, stored, hidden_state, wd, wg, wu, keys, values):
    toks, width = out_grad.shape
    ff = wd.shape[0]
    cw = width // 4
    n_rows = N_EXP * 36
    n_blk = N_EXP * MAIN
    pw = 2 * cw + cw // 4
    vm = pl.BlockSpec(memory_space=pltpu.VMEM)
    hbm = pl.BlockSpec(memory_space=pl.ANY)
    dma = pltpu.SemaphoreType.DMA
    slots = 8 + 3 * ZF
    back = 4 + 4 * RF
    rf = max(RF, 1)
    zf = max(ZF, 1)
    return pl.pallas_call(
        moe_kernel,
        out_shape=(
            jax.ShapeDtypeStruct((toks, width), BF),
            jax.ShapeDtypeStruct(keys.shape, BF),
            jax.ShapeDtypeStruct((3,) + keys.shape, BF),
            jax.ShapeDtypeStruct((3,) + keys.shape, BF),
        ),
        in_specs=[vm] * 4 + [hbm] * 5,
        out_specs=(vm, vm, hbm, hbm),
        scratch_shapes=[
            pltpu.VMEM((4, ff, cw), BF),
            pltpu.VMEM((width, ff), BF),
            pltpu.VMEM((width, ff), BF),
            pltpu.VMEM((4, 4, n_rows, cw), BF),
            pltpu.VMEM((3, n_rows, 2 * ff), BF),
            pltpu.VMEM((4, n_rows, ff), F32),
            pltpu.VMEM((4, n_rows, 2 * ff), BF),
            pltpu.VMEM((8, n_blk, pw), BF),
            pltpu.VMEM((slots, n_blk, pw), BF),
            pltpu.VMEM((back, n_blk, pw), BF),
            pltpu.VMEM((2, 4 - RF, n_rows // 2, cw), BF),
            pltpu.VMEM((2, 4 - RF, n_rows, cw), BF),
            pltpu.VMEM((2, rf, toks // 2, cw), BF),
            pltpu.VMEM((2, rf, toks, cw), BF),
            pltpu.VMEM((rf, 3, toks, cw), BF),
            pltpu.VMEM((2 * n_blk, 2 * toks), BF),
            pltpu.VMEM((4, n_blk, 2 * toks), BF),
            pltpu.VMEM((4, toks, 2 * n_blk), BF),
            pltpu.VMEM((4, 4, toks, n_blk), BF),
            pltpu.VMEM((3, zf, toks, cw), BF),
            pltpu.VMEM((3, 8, toks), F32),
            dma((6,)), dma((slots, 8)), dma((slots, 8)), dma((back, 8)), dma((back, 8)),
            dma((4, 2)), dma((4, 2)), dma((4, 2)), dma((4, 2)), dma((3,)), dma((3,)),
            dma((4, 2)), dma((4, 2)), dma((4, 2)), dma((4, 2)), dma((8,)), dma((8,)),
            dma((3,)), dma((3,)), dma((zf, 2)), dma((zf, 2)), dma((zf, 2)), dma((zf, 2)),
            dma((rf, 2)), dma((rf, 2)), dma((rf, 2)), dma((rf, 2)), dma((2, 3)), dma((2, 3)),
        ],
        compiler_params=pltpu.CompilerParams(
            collective_id=0, has_side_effects=True, vmem_limit_bytes=VMEM_LIMIT),
        cost_estimate=pl.CostEstimate(flops=15 * 10**9, bytes_accessed=20 * 10**6, transcendentals=0),
        name="moe",
    )(meta, out_grad, stored, hidden_state, wd, wg, wu, keys, values)


def attention_kernel(
    q_ref, go_ref, k_hbm, v_hbm, k_far, v_far, dq_ref, dk_ref, dv_ref,
    kv, probs, qt, mx, gs_t, g_rows, dqt, send, half_in, full_in,
    kv_sem, hs, hr, fs, fr_sem,
):
    fr = lax.axis_index("frame")
    left = lax.rem(fr + 3, 4)
    right = lax.rem(fr + 1, 4)
    span = q_ref.shape[0]
    scale = HD ** -0.5
    log2e = 1.4426950408889634

    def load(i, r):
        src = (k_hbm, v_hbm)[i] if isinstance(r, int) else (k_far, v_far)[i].at[r - 1]
        return pltpu.make_async_copy(src, kv.at[i, r], kv_sem.at[i, r])

    for i in range(2):
        load(i, 0).start()

    def load_far(r, carry):
        for i in range(2):
            load(i, r).start()
        return carry

    lax.fori_loop(1, fr + 1, load_far, 0)

    barrier = pltpu.get_barrier_semaphore()
    for dest in (left, right):
        pl.semaphore_signal(barrier, inc=1, device_id={"frame": dest}, device_id_type=MESH)
    pl.semaphore_wait(barrier, 2)

    def to_frame(src, dst, ss, rs, dest):
        return pltpu.make_async_remote_copy(
            src_ref=src, dst_ref=dst, send_sem=ss, recv_sem=rs,
            device_id={"frame": dest}, device_id_type=MESH)

    def half_copy(h):
        return to_frame(send.at[2, h], half_in.at[h], hs.at[h], hr.at[h], left if h == 0 else right)

    def full_copy(side, h):
        return to_frame(send.at[1 + 2 * side, h], full_in.at[side, h], fs.at[side, h], fr_sem.at[side, h],
                        left if side == 0 else right)

    def add_half(side, h):
        half_copy(h).wait_recv()
        for j in range(2):
            send[1 + 2 * side, h, j] = (
                send[1 + 2 * side, h, j].astype(F32) + half_in[h, j].astype(F32)).astype(BF)

    for i in range(2):
        load(i, 0).wait()

    def head(h, carry):
        cols = pl.ds(pl.multiple_of(h * HD, HD), HD)
        qt[...] = q_ref[:, cols].astype(F32).T.astype(BF)

        def forward(r, carry):
            @pl.when((r >= 1) & (h == 0))
            def _():
                for i in range(2):
                    load(i, r).wait()

            m, l, o = carry
            v_t = kv[1, r, :, cols].astype(F32).T.astype(BF)
            sc = dot_nn(kv[0, r, :, cols], qt[...])
            m_new = jnp.maximum(m, jnp.max(sc, axis=0, keepdims=True) * (scale * log2e))
            old = jnp.exp2(m - m_new)
            p = jnp.exp2(sc * (scale * log2e) - m_new)
            low = p.astype(BF)
            probs[r] = low
            mx[r] = m_new
            return m_new, l * old + jnp.sum(p, axis=0, keepdims=True), o * old + dot_nn(v_t, low)

        m, l, o = lax.fori_loop(0, fr + 1, forward, (
            jnp.full((1, span), -jnp.inf, F32), jnp.zeros((1, span), F32), jnp.zeros((HD, span), F32)))
        inv = 1.0 / l
        gs_t[...] = go_ref[:, cols].astype(F32).T * (inv * scale)
        centre = jnp.sum(gs_t[...] * (o * inv), axis=0, keepdims=True)
        dqt[...] = jnp.zeros_like(dqt)

        def backward(i, carry):
            r = jnp.where(i < 2, i + 2, 3 - i)

            @pl.when(r <= fr)
            def _():
                f = jnp.exp2(mx[r] - m)
                gt = (gs_t[...] * f).astype(BF)
                g_rows[...] = (gs_t[...] * (f * (1.0 / scale))).T.astype(BF)
                k_t = kv[0, r, :, cols].astype(F32).T.astype(BF)
                p = probs[r]
                dp = dot_nn(kv[1, r, :, cols], gt)
                ds = (p.astype(F32) * (dp - centre * f)).astype(BF)
                send[r, h, 0] = dot_nn(ds, q_ref[:, cols]).astype(BF)
                send[r, h, 1] = dot_nn(p, g_rows[...]).astype(BF)
                dqt[...] += dot_nn(k_t, ds)

            for h_at in range(2):
                @pl.when((i == 0) & (fr >= 2) & (h == h_at))
                def _():
                    half_copy(h_at).start()

            @pl.when((i == 1) & (fr == 3) & (h == 0))
            def _():
                full_copy(1, 0).start()

            @pl.when((i == 1) & (fr == 3) & (h == 1))
            def _():
                add_half(1, 1)
                full_copy(1, 1).start()

            @pl.when((i == 2) & (fr == 3) & (h == 0))
            def _():
                full_copy(0, 0).start()

            @pl.when((i == 2) & (fr >= 1) & (h == 1))
            def _():
                full_copy(0, 1).start()

            @pl.when((i == 2) & ((fr == 1) | (fr == 2)) & (h == 1))
            def _():
                add_half(0, 0)
                full_copy(0, 0).start()

            return carry

        lax.fori_loop(0, 4, backward, 0)
        dq_ref[:, cols] = dqt[...].T.astype(BF)
        return carry

    lax.fori_loop(0, 2, head, 0)

    @pl.when(fr == 0)
    def _():
        half_copy(1).wait_recv()
        send[3, 1] = half_in[1]
        full_copy(1, 1).start()

    def take(side, h):
        full_copy(side, h).wait_recv()
        for j in range(2):
            send[0, h, j] = (send[0, h, j].astype(F32) + full_in[side, h, j].astype(F32)).astype(BF)

    @pl.when(fr <= 2)
    def _():
        take(0, 1)
        take(0, 0)

    @pl.when(fr == 0)
    def _():
        take(1, 0)

    @pl.when(fr <= 1)
    def _():
        take(1, 1)

    for h in range(2):
        cols = pl.ds(h * HD, HD)
        dk_ref[:, cols] = send[0, h, 0]
        dv_ref[:, cols] = send[0, h, 1]

    for h in range(2):
        @pl.when(fr >= 2)
        def _():
            half_copy(h).wait_send()

        @pl.when(fr >= 1)
        def _():
            full_copy(0, h).wait_send()

    @pl.when(fr == 3)
    def _():
        full_copy(1, 0).wait_send()

    @pl.when((fr == 3) | (fr == 0))
    def _():
        full_copy(1, 1).wait_send()


def attention_call(q, go, k, v, k_far, v_far):
    span, width = q.shape
    vm = pl.BlockSpec(memory_space=pltpu.VMEM)
    hbm = pl.BlockSpec(memory_space=pl.ANY)
    dma = pltpu.SemaphoreType.DMA
    return pl.pallas_call(
        attention_kernel,
        out_shape=(jax.ShapeDtypeStruct(q.shape, BF),) * 3,
        in_specs=[vm] * 2 + [hbm] * 4,
        out_specs=(vm,) * 3,
        scratch_shapes=[
            pltpu.VMEM((2, 4, span, width), BF),
            pltpu.VMEM((4, span, span), BF),
            pltpu.VMEM((HD, span), BF),
            pltpu.VMEM((4, 1, span), F32),
            pltpu.VMEM((HD, span), F32),
            pltpu.VMEM((span, HD), BF),
            pltpu.VMEM((HD, span), F32),
            pltpu.VMEM((4, 2, 2, span, HD), BF),
            pltpu.VMEM((2, 2, span, HD), BF),
            pltpu.VMEM((2, 2, 2, span, HD), BF),
            dma((2, 4)), dma((2,)), dma((2,)), dma((2, 2)), dma((2, 2)),
        ],
        compiler_params=pltpu.CompilerParams(
            collective_id=1, has_side_effects=True, vmem_limit_bytes=VMEM_LIMIT),
        cost_estimate=pl.CostEstimate(flops=10 * 10**9, bytes_accessed=20 * 10**6, transcendentals=0),
        name="attention",
    )(q, go, k, v, k_far, v_far)


def on_device(
    queries, keys, values, hidden_state, out_grad, stored_pre, expert_ids, gate_weights,
    w_gate, w_up, w_down,
):
    toks = out_grad.shape[0]
    meta = jnp.concatenate(
        [expert_ids.astype(F32).T, gate_weights.T, jnp.zeros((4, toks), F32)], axis=0)
    resid, go, k_far, v_far = moe_call(
        meta, out_grad, stored_pre.reshape(toks, -1), hidden_state,
        w_down[0], w_gate[0], w_up[0], keys, values)
    dq, dk, dv = attention_call(queries, go, keys, values, k_far, v_far)
    return resid, dq, dk, dv


def solution(mesh):
    rows = P(("dp", "frame"), "expert")
    toks = ("dp", "frame", "expert")
    return jax.shard_map(
        on_device,
        mesh=mesh,
        in_specs=(
            rows, rows, rows, P(toks, None), P(toks, None), P(toks, None, None, None),
            P(toks, None), P(toks, None), P("expert", None, "frame"), P("expert", None, "frame"),
            P("expert", "frame", None),
        ),
        out_specs=(P(toks, None), rows, rows, rows),
        check_vma=False,
    )
```

profile of v0, /device:TPU:1, one launch (start us, length us, event | category | flops | bytes accessed | tf_op | source)
XLA Modules:
  0.0 279.6 jit_solution(12173691972263141291)
XLA Ops:
  0.6 0.1 pad.2.clone
  0.7 0.7 convert_bitcast_fusion
  1.4 1.3 maximum_maximum_fusion.meta_ref
  2.7 4.5 %reshape.11.st_ref = bf16[128,8192]{1,0:T(8,128)(2,1)} reshape(bf16[128,2,2,2048]{3,2,1,0:T(2,128)(2,1)} %param.16) | data formatting | bytes 4194304 | tf_op jit(solution)/shard_map/reshape | solution.py:832
  7.2 208.5 %moe.1 = (bf16[128,4096]{1,0:T(8,128)(2,1)}, bf16[1024,256]{1,0:T(8,128)(2,1)}, bf16[3,1024,256]{2,1,0:T(8,128)(2,1)}, bf16[3,1024,256]{2,1,0:T(8,128)(2,1)}) custom-call(f32[8,128]{1,0:T(8,128)} %maximum_maximum_fusion.meta_ref, bf16[128,4096]{1,0:T(8,128)(2,1)} %og_ref.1, bf16[128,8192]{1,0:T(8,128)(2,1)} %reshape.11.st_ref, bf16[128,4096]{1,0:T(8,128)(2,1)} %hs_ref.1, ...), custom_call_target="tpu_custom_call" | custom-call | flops 15000000512 | bytes 20000000 | tf_op jit(solution)/shard_map/moe/pallas_call | solution.py:571
  215.7 59.0 %attention.1 = (bf16[1024,256]{1,0:T(8,128)(2,1)}, bf16[1024,256]{1,0:T(8,128)(2,1)}, bf16[1024,256]{1,0:T(8,128)(2,1)}) custom-call(bf16[1024,256]{1,0:T(8,128)(2,1)} %q_ref.1, bf16[1024,256]{1,0:T(8,128)(2,1)} %get-tuple-element.12.go_ref, bf16[1024,256]{1,0:T(8,128)(2,1)} %k_hbm.3, bf16[1024,256]{1,0:T(8,128)(2,1)} %v_hbm.3, ...), custom_call_target="tpu_custom_call" | custom-call | flops 10000000000 | bytes 20000000 | tf_op jit(solution)/shard_map/attention/pallas_call | solution.py:799
  274.8 0.0 copy-start.2
  274.8 0.0 copy-start.1
  274.8 0.0 copy-start
  274.8 2.4 copy.19
  277.2 0.0 copy-done.2
  277.2 0.8 copy.20
  278.0 0.0 copy-done.1
  278.0 0.8 copy.21
  278.8 0.0 copy-done
  278.8 0.8 copy.22
  (1 shorter events, 0.0 us)
Async XLA Ops:
  274.8 2.4 copy-start.2
  274.8 3.2 %copy-start.1 = (bf16[1024,256]{1,0:T(8,128)(2,1)S(1)}, bf16[1024,256]{1,0:T(8,128)(2,1)}, u32[]{:S(2)}) copy-start(bf16[1024,256]{1,0:T(8,128)(2,1)} %get-tuple-element.24) | copy-start | bytes 1572868
  274.8 4.0 %copy-start = (bf16[1024,256]{1,0:T(8,128)(2,1)S(1)}, bf16[1024,256]{1,0:T(8,128)(2,1)}, u32[]{:S(2)}) copy-start(bf16[1024,256]{1,0:T(8,128)(2,1)} %get-tuple-element.25) | copy-start | bytes 1572868
where the time goes:
time: 280 us
  Pallas kernels  268 us (96%)
  local copies, waits for them, and re-layouts  9.33 us (3%)
    pallas_call x1, Pallas kernels, moe_call(): pl.pallas_call(moe_kernel, out_shape=(jax.ShapeDtypeStruct((toks, width),...  209 us
    pallas_call x1, Pallas kernels, attention_call(): pl.pallas_call(attention_kernel, out_shape=(jax.ShapeDtypeStruct(q.shape,...  59 us

commit v1 on v0

--- a/solution.py
+++ b/solution.py
@@ -160,7 +160,8 @@
 
     own_weights = routing(0, meta_ref[...])
 
-    def build_rows(c, carry):
+    def build_rows(i, carry):
+        c = lax.rem(i + ZF, 4)
         pack_tokens(c, c, og_ref[:, chunk_at(c)], own_weights)
         y_start(c, c)
         return carry
@@ -175,9 +176,9 @@
         y_start(4 + c, 4 + c)
         return carry
 
-    lax.fori_loop(ZF, 4, build_rows, 0)
+    lax.fori_loop(0, 4 - ZF, build_rows, 0)
     lax.fori_loop(0, 4, build_stored, 0)
-    lax.fori_loop(0, ZF, build_rows, 0)
+    lax.fori_loop(4 - ZF, 4, build_rows, 0)
 
     sel_r = lax.broadcasted_iota(jnp.int32, (4 * N_EXP, n_blk), 0)
     sel_c = lax.broadcasted_iota(jnp.int32, (4 * N_EXP, n_blk), 1)
@@ -217,18 +218,36 @@
 
     lax.fori_loop(ZF, 4, own_rows, 0)
 
+    def extra_block(n):
+        return lax.rem(n + 2, 3) + 1
+
+    def extra_slot(i):
+        return 2 + lax.rem(i, 6)
+
     for copy in meta_copies:
         copy.wait_recv()
-    for b in range(1, 4):
+
+    def dispatch(n, carry):
+        b = extra_block(n)
         weights = routing(b, meta_in[b - 1])
-        for c in range(ZF):
-            i = (b - 1) * ZF + c
-            if b == 3:
+
+        def one(c, carry):
+            i = n * ZF + c
+
+            @pl.when(n == 0)
+            def _():
                 for side in range(2):
                     raw_pass(c, side).wait_recv()
-            y_sent(i, i)
-            pack_tokens(i, 8 + i, raw[b - 1, c], weights)
-            y_start(i, 8 + i)
+
+            slot = extra_slot(i)
+            y_sent(slot, jnp.where(i < 6, slot, i + 2))
+            pack_tokens(slot, 8 + i, raw[b - 1, c], weights)
+            y_start(slot, 8 + i)
+            return carry
+
+        return lax.fori_loop(0, ZF, one, carry)
+
+    lax.fori_loop(0, 1, dispatch, 0)
 
     hid[...] = jnp.zeros_like(hid)
     for copy in w_copies[:4]:
@@ -238,10 +257,12 @@
         for side in range(2):
             ag_copy(c, side).wait_recv()
             fw_copy(c, side).start()
-        add_hidden(0, c)
-        add_hidden(1, c)
-        add_hidden(2, c)
-        return carry
+
+        def near(b, carry):
+            add_hidden(b, c)
+            return carry
+
+        return lax.fori_loop(0, 3, near, carry)
 
     lax.fori_loop(ZF, 4, next_rows, 0)
 
@@ -258,9 +279,7 @@
     for i in (2, 0, 1):
         st_copies[i].start()
 
-    for c in range(ZF):
-        unpack(c, c, rows.at[0, c])
-        add_hidden(0, c)
+    lax.fori_loop(1, 3, dispatch, 0)
 
     def far_rows(c, carry):
         for side in range(2):
@@ -270,11 +289,14 @@
 
     lax.fori_loop(ZF, 4, far_rows, 0)
 
-    for b in range(1, 4):
-        for c in range(ZF):
-            i = (b - 1) * ZF + c
-            unpack(i, 8 + i, rows.at[b, c])
-            add_hidden(b, c)
+    def dispatched(i, carry):
+        b = extra_block(i // ZF)
+        c = lax.rem(i, ZF)
+        unpack(extra_slot(i), 8 + i, rows.at[b, c])
+        add_hidden(b, c)
+        return carry
+
+    lax.fori_loop(0, ZF, dispatched, 0)
 
     def kv_near(i, side):
         src, dst = ((k_hbm, k_far), (v_hbm, v_far))[i]
@@ -284,29 +306,24 @@
         dst = (k_far, v_far)[i]
         return to_side(dst.at[2 * i], dst.at[1], kv_s.at[i, 2], kv_r.at[i, 2], i)
 
-    @pl.when(fr <= 2)
-    def _():
-        kv_near(0, 0).start()
-
-    @pl.when(fr == 0)
-    def _():
-        kv_near(0, 1).start()
-
     def hidden_to_grads(b, src):
-        h = hid[b]
-        g = src[:, pl.ds(0, ff)].astype(F32)
-        u = src[:, pl.ds(ff, ff)].astype(F32)
-        s = 1.0 / (1.0 + jnp.exp(-g))
-        gate = (h * u * s * (1.0 + g * (1.0 - s))).astype(BF)
-        up = (h * g * s).astype(BF)
-        grads[b, :, pl.ds(0, ff)] = gate
-        grads[b, :, pl.ds(ff, ff)] = up
-
-    for i in (2, 0, 1):
-        st_copies[i].wait()
-    for b in (3, 2, 1, 0):
-        hidden_to_grads(b, grads.at[0] if b == 0 else stored.at[b - 1])
-
+        def some_rows(i, carry):
+            at = pl.ds(pl.multiple_of(i * 32, 32), 32)
+            h = hid[b, at, :]
+            g = src[at, pl.ds(0, ff)].astype(F32)
+            u = src[at, pl.ds(ff, ff)].astype(F32)
+            s = 1.0 / (1.0 + jnp.exp(-g))
+            gate = (h * u * s * (1.0 + g * (1.0 - s))).astype(BF)
+            up = (h * g * s).astype(BF)
+            grads[b, at, pl.ds(0, ff)] = gate
+            grads[b, at, pl.ds(ff, ff)] = up
+            return carry
+
+        lax.fori_loop(0, n_rows // 32, some_rows, 0)
+
+    st_copies[2].wait()
+    st_copies[1].wait_send()
+    hidden_to_grads(3, stored.at[2])
     for copy in w_copies[4:]:
         copy.wait()
 
@@ -320,20 +337,6 @@
 
     def fu_copy(c, side):
         return to_side(rows.at[2 - side, c], full_in.at[side, c - RF], fu_s.at[c, side], fu_r.at[c, side], side)
-
-    def far_terms(c, carry):
-        rows[3, c] = term(3, c).astype(BF)
-        for side in range(2):
-            ha_copy(c, side).start()
-        return carry
-
-    lax.fori_loop(RF, 4, far_terms, 0)
-
-    def settle(i, carry):
-        y_sent(lax.rem(i, 8), i)
-        return carry
-
-    lax.fori_loop(n_extra, 8 + n_extra, settle, 0)
 
     def z_copy(slot, d):
         return to_expert(
@@ -352,6 +355,53 @@
         for d in range(1, N_EXP):
             z_copy(slot, d).start()
 
+    def far_terms(c, carry):
+        rows[3, c] = term(3, c).astype(BF)
+        for side in range(2):
+            ha_copy(c, side).start()
+        return carry
+
+    lax.fori_loop(RF, 4, far_terms, 0)
+    y_sent(0, 0)
+    send_back(0, term(3, 0).astype(BF))
+
+    @pl.when(fr <= 2)
+    def _():
+        kv_near(0, 0).start()
+
+    @pl.when(fr == 0)
+    def _():
+        kv_near(0, 1).start()
+
+    def own_dispatched(c, carry):
+        unpack(c, c, rows.at[0, c])
+        add_hidden(0, c)
+        return carry
+
+    lax.fori_loop(0, ZF, own_dispatched, 0)
+    lax.fori_loop(ZF, n_extra, dispatched, 0)
+    st_copies[0].wait()
+    st_copies[1].wait_recv()
+
+    def near_grads(i, carry):
+        hidden_to_grads(2 - i, stored.at[1 - i])
+        return carry
+
+    lax.fori_loop(0, 2, near_grads, 0)
+    hidden_to_grads(0, grads.at[0])
+
+    def settle(i, carry):
+        y_sent(i, i)
+        return carry
+
+    def settle_extra(i, carry):
+        y_sent(extra_slot(i), 8 + i)
+        return carry
+
+    lax.fori_loop(1, 2, settle, 0)
+    lax.fori_loop(2 + min(n_extra, 6), 8, settle, 0)
+    lax.fori_loop(max(n_extra - 6, 0), n_extra, settle_extra, 0)
+
     def tokens_of(slot, b):
         for d in range(1, N_EXP):
             z_copy(slot, d).wait_recv()
@@ -360,25 +410,37 @@
         extra = zrecv[slot, :, pl.ds(2 * cw, ext)]
         return got + jnp.concatenate([dot_nn(etmat[b, j], extra) for j in range(4)], axis=1)
 
-    for c in range(RF):
-        for b in (3, 2, 1, 0):
-            send_back(4 + 4 * c + b, term(b, c).astype(BF))
-
-    def near_terms(c, carry):
-        for side in range(2):
+    def near_terms(i, carry):
+        c = RF + i // 2
+        side = lax.rem(i, 2)
+
+        def block(side):
             @pl.when(c >= ZF)
             def _():
                 fw_copy(c, 1 - side).wait_send()
-            part = term(2 - side, c)
-            ha_copy(c, side).wait_recv()
-            lo = side * half
-            rows[2 - side, c, pl.ds(half - lo, half)] = part[half - lo:half - lo + half].astype(BF)
-            rows[2 - side, c, pl.ds(lo, half)] = (
-                part[lo:lo + half].astype(BF).astype(F32) + half_in[side, c - RF].astype(F32)).astype(BF)
-            fu_copy(c, side).start()
-        return carry
-
-    lax.fori_loop(RF, 4, near_terms, 0)
+
+        for side_at in range(2):
+            @pl.when(side == side_at)
+            def _():
+                block(side_at)
+
+        rows[2 - side, c] = term(2 - side, c).astype(BF)
+        for side_at in range(2):
+            @pl.when(side == side_at)
+            def _():
+                part = pl.ds(side_at * half, half)
+                ha_copy(c, side_at).wait_recv()
+                rows[2 - side_at, c, part] = (
+                    rows[2 - side_at, c, part].astype(F32) + half_in[side_at, c - RF].astype(F32)).astype(BF)
+                fu_copy(c, side_at).start()
+        return carry
+
+    def near_and_back(j, carry):
+        lax.fori_loop(2 * j, 2 * j + 2, near_terms, 0)
+        send_back(6 - j, term(2 - j, 0).astype(BF))
+        return carry
+
+    lax.fori_loop(0, 3, near_and_back, 0)
 
     def put_moe(c, got):
         hid[c, pl.ds(0, toks), :] = got[:, :cw // 2]
@@ -395,7 +457,7 @@
         return to_side(dense.at[c, 1 - side], dfull_in.at[side, c], df_s.at[c, side], df_r.at[c, side], side)
 
     for c in range(RF):
-        dense[c, 2] = tokens_of(4 + 4 * c + 3, 3).astype(BF)
+        dense[c, 2] = tokens_of(0, 3).astype(BF)
         for side in range(2):
             dh_copy(c, side).start()
         for side in range(2):
@@ -546,7 +608,7 @@
 
     lax.fori_loop(ZF, 4, drain, 0)
     lax.fori_loop(RF, 4, drain_back, 0)
-    lax.fori_loop(RF, 4 + 4 * RF, drain_z, 0)
+    lax.fori_loop(0, 7, drain_z, 0)
     for c in range(ZF, RF):
         for side in range(2):
             fw_copy(c, side).wait_send()
@@ -565,7 +627,7 @@
     hbm = pl.BlockSpec(memory_space=pl.ANY)
     dma = pltpu.SemaphoreType.DMA
     slots = 8 + 3 * ZF
-    back = 4 + 4 * RF
+    back = 7
     rf = max(RF, 1)
     zf = max(ZF, 1)
     return pl.pallas_call(

time: 280 us -> 267 us (0.954)
  Pallas kernels: 268 us -> 255 us
    pallas_call x1, Pallas kernels: 209 us -> 193 us  [moe_call(): pl.pallas_call(moe_kernel, out_shape=(jax.ShapeDtypeStruct((toks, width),...]
where the time goes in v1:
time: 267 us
  Pallas kernels  255 us (96%)
  local copies, waits for them, and re-layouts  9.33 us (3%)
    pallas_call x1, Pallas kernels, moe_call(): pl.pallas_call(moe_kernel, out_shape=(jax.ShapeDtypeStruct((toks, width),...  193 us
    pallas_call x1, Pallas kernels, attention_call(): pl.pallas_call(attention_kernel, out_shape=(jax.ShapeDtypeStruct(q.shape,...  61.8 us

profile of v1, /device:TPU:1, one launch (start us, length us, event | category | flops | bytes accessed | tf_op | source)
XLA Modules:
  0.0 266.6 jit_solution(7426292821887603392)
XLA Ops:
  0.6 0.1 pad.2.clone
  0.7 0.7 convert_bitcast_fusion
  1.4 1.3 maximum_maximum_fusion.meta_ref
  2.7 4.5 %reshape.11.st_ref = bf16[128,8192]{1,0:T(8,128)(2,1)} reshape(bf16[128,2,2,2048]{3,2,1,0:T(2,128)(2,1)} %param.16) | data formatting | bytes 4194304 | tf_op jit(solution)/shard_map/reshape | solution.py:894
  7.2 192.8 %moe.1 = (bf16[128,4096]{1,0:T(8,128)(2,1)}, bf16[1024,256]{1,0:T(8,128)(2,1)}, bf16[3,1024,256]{2,1,0:T(8,128)(2,1)}, bf16[3,1024,256]{2,1,0:T(8,128)(2,1)}) custom-call(f32[8,128]{1,0:T(8,128)} %maximum_maximum_fusion.meta_ref, bf16[128,4096]{1,0:T(8,128)(2,1)} %og_ref.1, bf16[128,8192]{1,0:T(8,128)(2,1)} %reshape.11.st_ref, bf16[128,4096]{1,0:T(8,128)(2,1)} %hs_ref.1, ...), custom_call_target="tpu_custom_call" | custom-call | flops 15000000512 | bytes 20000000 | tf_op jit(solution)/shard_map/moe/pallas_call | solution.py:633
  200.0 61.8 %attention.1 = (bf16[1024,256]{1,0:T(8,128)(2,1)}, bf16[1024,256]{1,0:T(8,128)(2,1)}, bf16[1024,256]{1,0:T(8,128)(2,1)}) custom-call(bf16[1024,256]{1,0:T(8,128)(2,1)} %q_ref.1, bf16[1024,256]{1,0:T(8,128)(2,1)} %get-tuple-element.12.go_ref, bf16[1024,256]{1,0:T(8,128)(2,1)} %k_hbm.3, bf16[1024,256]{1,0:T(8,128)(2,1)} %v_hbm.3, ...), custom_call_target="tpu_custom_call" | custom-call | flops 10000000000 | bytes 20000000 | tf_op jit(solution)/shard_map/attention/pallas_call | solution.py:861
  261.8 0.0 copy-start.2
  261.8 0.0 copy-start.1
  261.8 0.0 copy-start
  261.8 2.4 copy.19
  264.2 0.0 copy-done.2
  264.2 0.8 copy.20
  265.0 0.0 copy-done.1
  265.0 0.8 copy.21
  265.8 0.0 copy-done
  265.8 0.8 copy.22
  (1 shorter events, 0.0 us)
Async XLA Ops:
  261.8 2.4 copy-start.2
  261.8 3.2 %copy-start.1 = (bf16[1024,256]{1,0:T(8,128)(2,1)S(1)}, bf16[1024,256]{1,0:T(8,128)(2,1)}, u32[]{:S(2)}) copy-start(bf16[1024,256]{1,0:T(8,128)(2,1)} %get-tuple-element.24) | copy-start | bytes 1572868
  261.8 4.0 %copy-start = (bf16[1024,256]{1,0:T(8,128)(2,1)S(1)}, bf16[1024,256]{1,0:T(8,128)(2,1)}, u32[]{:S(2)}) copy-start(bf16[1024,256]{1,0:T(8,128)(2,1)} %get-tuple-element.25) | copy-start | bytes 1572868

commit v2 on v1

--- a/solution.py
+++ b/solution.py
@@ -30,7 +30,7 @@
 
 
 def moe_kernel(
-    meta_ref, og_ref, st_ref, hs_ref, wd_hbm, wg_hbm, wu_hbm, k_hbm, v_hbm,
+    meta_ref, og_ref, st_ref, hs_ref, wd_hbm, wg_hbm, wu_hbm, k_ref, v_ref,
     resid_ref, gout_ref, k_far, v_far,
     wd, wg, wu, rows, stored, hid, grads, ysend, yrecv, zrecv,
     half_in, full_in, dhalf_in, dfull_in, dense, amat, emat, atmat, etmat, raw, meta_in,
@@ -299,7 +299,7 @@
     lax.fori_loop(0, ZF, dispatched, 0)
 
     def kv_near(i, side):
-        src, dst = ((k_hbm, k_far), (v_hbm, v_far))[i]
+        src, dst = ((k_ref, k_far), (v_ref, v_far))[i]
         return to_side(src, dst.at[2 * side], kv_s.at[i, side], kv_r.at[i, side], side)
 
     def kv_pass(i):
@@ -638,7 +638,7 @@
             jax.ShapeDtypeStruct((3,) + keys.shape, BF),
             jax.ShapeDtypeStruct((3,) + keys.shape, BF),
         ),
-        in_specs=[vm] * 4 + [hbm] * 5,
+        in_specs=[vm] * 4 + [hbm] * 3 + [vm] * 2,
         out_specs=(vm, vm, hbm, hbm),
         scratch_shapes=[
             pltpu.VMEM((4, ff, cw), BF),

time: 267 us -> 267 us (level)
  no operation moved by 1% of the time
where the time goes in v2:
time: 267 us
  Pallas kernels  255 us (96%)
  local copies, waits for them, and re-layouts  9.33 us (3%)
    pallas_call x1, Pallas kernels, moe_call(): pl.pallas_call(moe_kernel, out_shape=(jax.ShapeDtypeStruct((toks, width),...  193 us
    pallas_call x1, Pallas kernels, attention_call(): pl.pallas_call(attention_kernel, out_shape=(jax.ShapeDtypeStruct(q.shape,...  61.8 us

profile of v2, /device:TPU:1, one launch (start us, length us, event | category | flops | bytes accessed | tf_op | source)
XLA Modules:
  0.0 266.9 jit_solution(566734478731788409)
XLA Ops:
  0.6 0.1 pad.2.clone
  0.7 0.7 convert_bitcast_fusion
  1.4 1.3 maximum_maximum_fusion.meta_ref
  2.7 4.5 %reshape.11.st_ref = bf16[128,8192]{1,0:T(8,128)(2,1)} reshape(bf16[128,2,2,2048]{3,2,1,0:T(2,128)(2,1)} %param.16) | data formatting | bytes 4194304 | tf_op jit(solution)/shard_map/reshape | solution.py:894
  7.2 193.1 %moe.1 = (bf16[128,4096]{1,0:T(8,128)(2,1)}, bf16[1024,256]{1,0:T(8,128)(2,1)}, bf16[3,1024,256]{2,1,0:T(8,128)(2,1)}, bf16[3,1024,256]{2,1,0:T(8,128)(2,1)}) custom-call(f32[8,128]{1,0:T(8,128)} %maximum_maximum_fusion.meta_ref, bf16[128,4096]{1,0:T(8,128)(2,1)} %og_ref.1, bf16[128,8192]{1,0:T(8,128)(2,1)} %reshape.11.st_ref, bf16[128,4096]{1,0:T(8,128)(2,1)} %hs_ref.1, ...), custom_call_target="tpu_custom_call" | custom-call | flops 15000000512 | bytes 20000000 | tf_op jit(solution)/shard_map/moe/pallas_call | solution.py:633
  200.3 61.8 %attention.1 = (bf16[1024,256]{1,0:T(8,128)(2,1)}, bf16[1024,256]{1,0:T(8,128)(2,1)}, bf16[1024,256]{1,0:T(8,128)(2,1)}) custom-call(bf16[1024,256]{1,0:T(8,128)(2,1)} %q_ref.1, bf16[1024,256]{1,0:T(8,128)(2,1)} %get-tuple-element.12.go_ref, bf16[1024,256]{1,0:T(8,128)(2,1)} %k_hbm.1, bf16[1024,256]{1,0:T(8,128)(2,1)} %v_hbm.1, ...), custom_call_target="tpu_custom_call" | custom-call | flops 10000000000 | bytes 20000000 | tf_op jit(solution)/shard_map/attention/pallas_call | solution.py:861
  262.1 0.0 copy-start.2
  262.1 0.0 copy-start.1
  262.1 0.0 copy-start
  262.1 2.4 copy.19
  264.5 0.0 copy-done.2
  264.5 0.8 copy.20
  265.3 0.0 copy-done.1
  265.3 0.8 copy.21
  266.1 0.0 copy-done
  266.1 0.8 copy.22
  (1 shorter events, 0.0 us)
Async XLA Ops:
  262.1 2.4 copy-start.2
  262.1 3.2 %copy-start.1 = (bf16[1024,256]{1,0:T(8,128)(2,1)S(1)}, bf16[1024,256]{1,0:T(8,128)(2,1)}, u32[]{:S(2)}) copy-start(bf16[1024,256]{1,0:T(8,128)(2,1)} %get-tuple-element.24) | copy-start | bytes 1572868
  262.1 4.0 %copy-start = (bf16[1024,256]{1,0:T(8,128)(2,1)S(1)}, bf16[1024,256]{1,0:T(8,128)(2,1)}, u32[]{:S(2)}) copy-start(bf16[1024,256]{1,0:T(8,128)(2,1)} %get-tuple-element.25) | copy-start | bytes 1572868
